TPU v7x, 512 devices: a whole 4x4x16 slice. The times are simulated.
512 devices in a mesh: ens: 16 (over x_hi, y, core), space: 32 (over x_lo, z).
Axes of the slice: x: 4 (x_hi: 2, x_lo: 2; x = x_hi * 2 + x_lo), y: 4, z: 16, core: 2. Of those that a mesh axis runs over, the one named last changes fastest.
Arguments:
- ensemble: bfloat16 [128, 2, 1024, 512], P('ens', None, 'space'), may hold values from -6 to 6
- control: float32 [128, 2, 1024, 512], P('ens', None, 'space'), may hold values from -6 to 6
- spectrum: float32 [2, 512, 1024], P(None, 'space'), may hold values from 0.1 to 2
- row_scale: float32 [2, 1024], P(None, 'space'), may hold values from 0.5 to 2
- precision: float32 [2, 1024, 512], P(None, 'space'), may hold values from 0.5 to 8
- innovation: float32 [2, 1024, 512], P(None, 'space'), may hold values from -6 to 6
Outputs:
- gradient: float32 [128, 2, 1024, 512], P('ens', None, 'space')
All inputs are finite; a program needn't handle non-finite values.
Results may differ from a plain program's by a relative error of at most 0.0003.
Values sent between devices are 32-bit elements; how exact they have to be, the bound alone decides.
A program may use at most 64 MiB of HBM per device.

v0:
```python
import math

import jax
import jax.numpy as jnp
from jax import lax
from jax.sharding import PartitionSpec as P

HIGH = lax.Precision.HIGHEST


def hartley_table(length):
    index = jnp.arange(length, dtype=jnp.int32)
    product = index[:, None] * index[None, :] % length
    angle = product.astype(jnp.float32) * (2.0 * math.pi / length)
    return (jnp.cos(angle) + jnp.sin(angle)) / math.sqrt(length)


def localize(fields, spectrum, col_table, row_table):
    columns = jnp.einsum("mlrc,ck->mlkr", fields, col_table, precision=HIGH)
    columns = lax.all_to_all(columns, "space", split_axis=2, concat_axis=3, tiled=True)
    rows = jnp.einsum("mlkr,rq->mlkq", columns, row_table, precision=HIGH) * spectrum[None]
    rows = jnp.einsum("mlkq,qr->mlkr", rows, row_table, precision=HIGH)
    rows = lax.all_to_all(rows, "space", split_axis=3, concat_axis=2, tiled=True)
    return jnp.einsum("mlkr,kc->mlrc", rows, col_table, precision=HIGH)


def body(ensemble, control, spectrum, row_scale, precision, innovation):
    members_all = ensemble.shape[0] * lax.axis_size("ens")
    col_table = hartley_table(control.shape[3])
    row_table = hartley_table(spectrum.shape[2])
    members = ensemble.astype(jnp.float32)
    alpha = localize(control, spectrum, col_table, row_table)
    scale = row_scale[:, :, None] * (1.0 / math.sqrt(members_all - 1))
    partial_sum = jnp.sum(members * alpha, axis=0)
    total = lax.psum(partial_sum, "ens")
    weighted = precision * (scale * total - innovation)
    adjoint_in = members * (scale * weighted)[None]
    return control + localize(adjoint_in, spectrum, col_table, row_table)


def solution(mesh):
    in_specs = (
        P("ens", None, "space", None),
        P("ens", None, "space", None),
        P(None, "space", None),
        P(None, "space"),
        P(None, "space", None),
        P(None, "space", None),
    )
    out_specs = P("ens", None, "space", None)
    return jax.shard_map(body, mesh=mesh, in_specs=in_specs, out_specs=out_specs, check_vma=False)
```

profile of v0, /device:TPU:1, one launch (start us, length us, event | category | flops | bytes accessed | tf_op | source)
XLA Modules:
  0.0 709.2 jit_solution(8596363719077343833)
XLA Ops:
  6.5 7.9 %convolution_bitcast_fusion.1 = f32[8,2,512,32]{2,3,1,0:T(8,128)S(1)} fusion(f32[8,2,32,512]{3,2,1,0:T(8,128)} %param.7), kind=kOutput, calls=%fused_computation.24 | convolution fusion | flops 1614807040 | bytes 2097152 | tf_op jit(solution)/shard_map/mlrc,ck->mlkr/dot_general | solution.py:19
  18.9 5.8 reshape.6
  24.7 66.6 %all_to_all.72 = f32[32,1,8192]{2,1,0:T(1,128)S(1)} all-to-all(f32[32,1,8192]{2,1,0:T(1,128)S(1)} %reshape.6), channel_id=1, replica_groups=mesh['ens'=16,'space'=32] {'space'}, dimensions={0} | all-to-all | bytes 2097152 | tf_op jit(solution)/shard_map/all_to_all | solution.py:20
  95.1 4.9 reshape.7
  110.5 21.5 %fusion.14 = f32[8,2,16,1024]{3,2,1,0:T(8,128)S(1)} fusion(f32[8,2,16,1024]{3,2,1,0:T(8,128)S(1)} %all_to_all.55, f32[2,16,1024]{2,1,0:T(8,128)S(1)} %copy-done.5), kind=kOutput, calls=%fused_computation.25 | convolution fusion | flops 3238264832 | bytes 2228224 | tf_op jit(solution)/shard_map/mlkr,rq->mlkq/dot_general | solution.py:21
  132.0 21.4 %fusion.7 = f32[8,2,16,1024]{3,2,1,0:T(8,128)S(1)} fusion(f32[8,2,16,1024]{3,2,1,0:T(8,128)S(1)} %fusion.14), kind=kOutput, calls=%fused_computation.10 | convolution fusion | flops 3238002688 | bytes 2097152 | tf_op jit(solution)/shard_map/mlkq,qr->mlkr/dot_general | solution.py:22
  153.5 8.7 %copy.18 = f32[8,2,16,1024]{2,1,0,3:T(2,128)} copy(f32[8,2,16,1024]{3,2,1,0:T(8,128)S(1)} %fusion.7) | data formatting | bytes 2097152 | tf_op jit(solution)/shard_map/mlkq,qr->mlkr/dot_general | solution.py:22
  162.2 13.2 %reshape.8 = f32[32,1,8192]{2,1,0:T(1,128)S(1)} reshape(f32[1024,8,2,16]{3,2,1,0:T(2,128)} %bitcast.63) | data formatting | bytes 2097152
  175.3 59.1 %all_to_all.73 = f32[32,1,8192]{2,1,0:T(1,128)S(1)} all-to-all(f32[32,1,8192]{2,1,0:T(1,128)S(1)} %reshape.8), channel_id=1, replica_groups=mesh['ens'=16,'space'=32] {'space'}, dimensions={0} | all-to-all | bytes 2097152 | tf_op jit(solution)/shard_map/all_to_all | solution.py:23
  237.6 12.6 %reshape.9 = f32[1024,8,2,16]{3,2,1,0:T(2,128)} reshape(f32[32,8192]{1,0:T(8,128)S(1)} %reduce.1) | data formatting | bytes 2097152
  250.2 11.6 %copy.19 = f32[8,2,16,32,32]{4,2,3,1,0:T(8,128)} copy(f32[8,2,16,32,32]{2,1,0,4,3:T(2,128)} %bitcast.64) | data formatting | bytes 2097152 | tf_op jit(solution)/shard_map/all_to_all | solution.py:23
  261.7 20.1 %fusion.20 = f32[2,32,512]{2,1,0:T(8,128)} fusion(f32[8,2,512,32]{3,2,1,0:T(8,128)} %bitcast.74, bf16[8,2,32,512]{3,2,1,0:T(8,128)(2,1)S(1)} %copy-done.4), kind=kOutput, calls=%fused_computation.28 | convolution fusion | flops 1615560704 | bytes 1703936 | tf_op jit(solution)/shard_map/mlkr,kc->mlrc/dot_general | solution.py:24
  281.8 150.2 %all-reduce.2.cloned.1.call-done = f32[2,32,512]{2,1,0:T(8,128)} async-done(((f32[2,32,512]{2,1,0:T(8,128)}), f32[2,32,512]{2,1,0:T(8,128)}) %all-reduce.2.cloned.1.call-update) | async-done | bytes 131088 | tf_op jit(solution)/shard_map/psum | solution.py:35
  433.0 6.9 convolution_bitcast_fusion
  444.4 5.8 reshape.10
  450.2 62.4 %all_to_all.74 = f32[32,1,8192]{2,1,0:T(1,128)S(1)} all-to-all(f32[32,1,8192]{2,1,0:T(1,128)S(1)} %reshape.10), channel_id=1, replica_groups=mesh['ens'=16,'space'=32] {'space'}, dimensions={0} | all-to-all | bytes 2097152 | tf_op jit(solution)/shard_map/all_to_all | solution.py:20
  531.1 21.7 %fusion.17 = f32[8,2,16,1024]{3,2,1,0:T(8,128)S(1)} fusion(f32[8,2,16,1024]{3,2,1,0:T(8,128)S(1)} %all_to_all.63, f32[2,16,1024]{2,1,0:T(8,128)S(1)} %copy-done.5), kind=kOutput, calls=%fused_computation.26 | convolution fusion | flops 3238264832 | bytes 2228224 | tf_op jit(solution)/shard_map/mlkr,rq->mlkq/dot_general | solution.py:21
  552.9 21.4 %fusion.3 = f32[8,2,16,1024]{3,2,1,0:T(8,128)S(1)} fusion(f32[8,2,16,1024]{3,2,1,0:T(8,128)S(1)} %fusion.17), kind=kOutput, calls=%fused_computation.6 | convolution fusion | flops 3238002688 | bytes 2097152 | tf_op jit(solution)/shard_map/mlkq,qr->mlkr/dot_general | solution.py:22
  574.3 8.7 %copy.24 = f32[8,2,16,1024]{2,1,0,3:T(2,128)} copy(f32[8,2,16,1024]{3,2,1,0:T(8,128)S(1)} %fusion.3) | data formatting | bytes 2097152 | tf_op jit(solution)/shard_map/mlkq,qr->mlkr/dot_general | solution.py:22
  583.0 13.2 %reshape.12 = f32[32,1,8192]{2,1,0:T(1,128)S(1)} reshape(f32[1024,8,2,16]{3,2,1,0:T(2,128)} %bitcast.65) | data formatting | bytes 2097152
  596.2 58.5 %all_to_all.75 = f32[32,1,8192]{2,1,0:T(1,128)S(1)} all-to-all(f32[32,1,8192]{2,1,0:T(1,128)S(1)} %reshape.12), channel_id=1, replica_groups=mesh['ens'=16,'space'=32] {'space'}, dimensions={0} | all-to-all | bytes 2097152 | tf_op jit(solution)/shard_map/all_to_all | solution.py:23
  657.9 12.6 %reshape.13 = f32[1024,8,2,16]{3,2,1,0:T(2,128)} reshape(f32[32,8192]{1,0:T(8,128)S(1)} %reduce.3) | data formatting | bytes 2097152
  670.4 11.6 %copy.25 = f32[8,2,16,32,32]{4,2,3,1,0:T(8,128)} copy(f32[8,2,16,32,32]{2,1,0,4,3:T(2,128)} %bitcast.66) | data formatting | bytes 2097152 | tf_op jit(solution)/shard_map/all_to_all | solution.py:23
  682.0 20.1 %convolution_add_fusion = f32[8,2,32,512]{3,2,1,0:T(8,128)} fusion(f32[8,2,32,512]{3,2,1,0:T(8,128)S(1)} %copy-done, f32[8,2,512,32]{3,2,1,0:T(8,128)} %bitcast.69), kind=kOutput, calls=%fused_computation.21 | convolution fusion | flops 1615069184 | bytes 3145728 | tf_op jit(solution)/shard_map/mlkr,kc->mlrc/dot_general | solution.py:24
  (30 shorter events, 49.1 us)
Async XLA Ops:
  6.5 425.5 %all-reduce.2.cloned.1.call-start = ((), (), s32[]{:S(2)}) async-start(), calls=%async_computation.4 | async-start | bytes 262144 | tf_op jit(solution)/shard_map/psum | solution.py:35
  106.7 3.8 copy-start.5
  250.2 11.6 %copy-start.4 = (bf16[8,2,32,512]{3,2,1,0:T(8,128)(2,1)S(1)}, bf16[8,2,32,512]{3,2,1,0:T(8,128)(2,1)}, u32[]{:S(2)}) copy-start(bf16[8,2,32,512]{3,2,1,0:T(8,128)(2,1)} %param.6) | copy-start | bytes 1572868
  261.7 20.1 %copy-start.3 = (f32[2,32]{1,0:T(2,128)S(1)}, f32[2,32]{1,0:T(2,128)}, u32[]{:S(2)}) copy-start(f32[2,32]{1,0:T(2,128)} %param.9) | copy-start | bytes 772
  261.7 170.3 %copy-start.1 = (f32[2,32,512]{2,1,0:T(8,128)S(1)}, f32[2,32,512]{2,1,0:T(8,128)}, u32[]{:S(2)}) copy-start(f32[2,32,512]{2,1,0:T(8,128)} %param.10) | copy-start | bytes 393220
  261.7 170.3 %copy-start.2 = (f32[2,32,512]{2,1,0:T(8,128)S(1)}, f32[2,32,512]{2,1,0:T(8,128)}, u32[]{:S(2)}) copy-start(f32[2,32,512]{2,1,0:T(8,128)} %param.11) | copy-start | bytes 393220
  670.4 11.6 %copy-start = (f32[8,2,32,512]{3,2,1,0:T(8,128)S(1)}, f32[8,2,32,512]{3,2,1,0:T(8,128)}, u32[]{:S(2)}) copy-start(f32[8,2,32,512]{3,2,1,0:T(8,128)} %param.7) | copy-start | bytes 3145732
Sparse Core Ops, SparseCore 0:
  281.9 150.0 all-reduce.1
where the time goes:
time: 720 us; the launch traced here: 709 us
  blocking collectives  247 us (34%)
  waiting for transfers between devices  150 us (21%)
  local copies, waits for them, and re-layouts  144 us (20%)
  matrix products  141 us (20%)
  between operations  13.8 us (2%)
  other arithmetic  13.7 us (2%)
    psum x1, waiting for transfers between devices, body(): total = lax.psum(partial_sum, 'ens')  150 us
    all_to_all x2, blocking collectives, localize(): lax.all_to_all(columns, 'space', split_axis=2, concat_axis=3, tiled=True)  129 us
    all_to_all x2, blocking collectives, localize(): lax.all_to_all(rows, 'space', split_axis=3, concat_axis=2, tiled=True)  118 us
    unnamed x20, local copies, waits for them, and re-layouts  72.8 us
    dot_general x2, matrix products, localize(): jnp.einsum('mlkr,rq->mlkq', columns, row_table, precision=HIGH)  43.3 us
    dot_general x2, matrix products, localize(): rows = jnp.einsum('mlkq,qr->mlkr', rows, row_table, precision=HIGH)  42.8 us
    dot_general x2, matrix products, localize(): return jnp.einsum('mlkr,kc->mlrc', rows, col_table, precision=HIGH)  40.2 us
    all_to_all x2, local copies, waits for them, and re-layouts, localize(): lax.all_to_all(rows, 'space', split_axis=3, concat_axis=2, tiled=True)  23.2 us
  transfers between devices with their start and end apart: 1, of which 1 were waited for; matrix products, arithmetic and copies ran while one was open for 0% of the time, Pallas kernels for 0%

commit v1 on v0

v1 whole, which is shorter than its diff:
```python
import functools
import math

import jax
import jax.numpy as jnp
import ml_dtypes
import numpy as np
from jax import lax
from jax.experimental import pallas as pl
from jax.experimental.pallas import tpu as pltpu
from jax.sharding import PartitionSpec as P

MESH = pl.DeviceIdType.MESH
SPZ, SPG, C, E, GX, RS1, RS2, WZ, WG, AX, G = range(11)


def hartley_matrix(n):
    index = np.arange(n, dtype=np.int64)
    angle = (index[:, None] * index[None, :] % n) * (2.0 * math.pi / n)
    return (np.cos(angle) + np.sin(angle)) / math.sqrt(n)


def two_parts(table):
    high = table.astype(ml_dtypes.bfloat16)
    low = (table - high.astype(np.float64)).astype(ml_dtypes.bfloat16)
    return np.stack([high, low])


def dot(a, b):
    return jnp.dot(a, b, preferred_element_type=jnp.float32)


def parts_of(x):
    high = x.astype(jnp.bfloat16)
    return high, (x - high.astype(jnp.float32)).astype(jnp.bfloat16)


def times_table(x, table):
    high, low = parts_of(x)
    return dot(high, table[0]) + dot(low, table[0]) + dot(high, table[1])


def table_times(table, k, y):
    high, low = parts_of(y)
    width = y.shape[1]
    both = dot(table[k, 0], jnp.concatenate([high, low], axis=1))
    return both[:, :width] + both[:, width:] + dot(table[k, 1], high)


def kernel(
    zn, jn, factor,
    ctrl, ens, spec, rscale, prec, innov, col, icol, row_hbm,
    out,
    row, cst, crecv, e32, erecv, specz, specg, spect, field, gx, prod, rs1, part, rs2, wz, wg, adj, adjc, ax, gout, grecv,
    send, recv, local_sem,
):
    mn, _, rn, ny = ctrl.shape
    nx = spec.shape[2]
    kb = spec.shape[1] // 2
    kc = ny // 4
    hr = rn // 2
    half = nx // 2
    an, bn = prod.shape[1] // (ny // prod.shape[4]), ny // prod.shape[4]
    lw = prod.shape[4]
    px = nx // jn
    ei, si = lax.axis_index("ens"), lax.axis_index("space")
    j, core = lax.div(ei, 2), lax.rem(ei, 2)
    xl, z = lax.div(si, zn), lax.rem(si, zn)
    q = xl * 2 + core
    owner_core = lax.div(z, mn)
    member = lax.rem(z, mn)
    in_plane_set = owner_core == core

    def dev(j_, xl_, core_, z_):
        return (j_ * 2 + core_, xl_ * zn + z_)

    def remote(src, dst, phase, l, device):
        return pltpu.make_async_remote_copy(
            src_ref=src, dst_ref=dst, send_sem=send.at[phase, l], recv_sem=recv.at[phase, l],
            device_id=device, device_id_type=MESH,
        )

    def wait(sem, ref):
        pltpu.make_async_copy(ref, ref, sem).wait()

    barrier = pltpu.get_barrier_semaphore()
    mine = q * zn + z

    def greet_group(t, _):
        other = lax.rem(mine + t, 4 * zn)
        oq, oz = lax.div(other, zn), lax.rem(other, zn)
        pl.semaphore_signal(barrier, inc=1, device_id=dev(j, lax.div(oq, 2), lax.rem(oq, 2), oz), device_id_type=MESH)
        return 0

    lax.fori_loop(1, 4 * zn, greet_group, 0)

    def greet_others(t, _):
        pl.semaphore_signal(barrier, inc=1, device_id=dev(lax.rem(j + t, jn), xl, core, z), device_id_type=MESH)
        return 0

    lax.fori_loop(1, jn, greet_others, 0)
    row_copy = pltpu.make_async_copy(row_hbm, row, local_sem)
    row_copy.start()

    def prepare(l, _):
        x = ctrl[:, l].reshape(mn * rn, ny)
        y = times_table(x, col)
        for k in range(4):
            cst[l, :, k] = y[:, k * kc : (k + 1) * kc].reshape(mn, rn, kc)
        for m in range(mn):
            e32[l, m] = ens[m, l].astype(jnp.float32).reshape(2, an, 8, ny)
        return 0

    lax.fori_loop(0, 2, prepare, 0)
    core_k = pl.multiple_of(core * kb, kb)
    piece = pl.multiple_of(j * px, px)
    specz[:, z] = spec[:, pl.ds(core_k, kb), pl.ds(piece, px)]

    pl.semaphore_wait(barrier, 4 * zn - 1 + jn - 1)

    def send_spec(t, _):
        remote(specz.at[:, z], specz.at[:, z], SPZ, 0, dev(j, xl, core, lax.rem(z + t, zn))).start()
        return 0

    lax.fori_loop(1, zn, send_spec, 0)

    def either(same, src, dst, phase, l, device):
        @pl.when(same)
        def _():
            pltpu.make_async_copy(src, dst, recv.at[phase, l]).start()

        @pl.when(jnp.logical_not(same))
        def _():
            remote(src, dst, phase, l, device).start()

    def send_inputs(l, _):
        def send_c(t, _):
            m = lax.rem(lax.div(t, 4) + z, mn)
            k = lax.rem(t, 4)
            xd, cd, zd = lax.div(k, 2), lax.rem(k, 2), core * mn + m
            same = (k == q) & (zd == z)
            either(same, cst.at[l, m, k], crecv.at[l, xl, z], C, l, dev(j, xd, cd, zd))
            return 0

        lax.fori_loop(0, 4 * mn, send_c, 0)

        def send_e(t, _):
            m = lax.rem(lax.div(t, 2) + z, mn)
            cd, zd = lax.rem(t, 2), core * mn + m
            same = (cd == core) & (zd == z)
            either(same, e32.at[l, m, cd], erecv.at[l, z], E, l, dev(j, xl, cd, zd))
            return 0

        lax.fori_loop(0, 2 * mn, send_e, 0)
        return 0

    lax.fori_loop(0, 2, send_inputs, 0)

    wait(recv.at[SPZ, 0], specz.at[:, pl.ds(0, zn - 1)])

    def to_groups(src, dst, phase, l):
        def one(t, _):
            remote(src, dst, phase, l, dev(lax.rem(j + t, jn), xl, core, z)).start()
            return 0

        lax.fori_loop(1, jn, one, 0)

    to_groups(specz, specg.at[j], SPG, 0)
    specg[j] = specz[...]
    row_copy.wait()
    wait(recv.at[SPG, 0], specg.at[pl.ds(0, jn - 1)])
    for l in range(2):
        for k in range(jn):
            spect[l, k * px : (k + 1) * px] = specg[k, l].reshape(kc, px).T

    def rows(l, y):
        even = table_times(row, 0, y[:half] + y[half:]) * spect[l, pl.ds(0, half, 2), :]
        odd = table_times(row, 1, y[:half] - y[half:]) * spect[l, pl.ds(1, half, 2), :]
        a = table_times(row, 0, even)
        b = table_times(row, 2, odd)
        return a + b, a - b

    def to_plane(src_of, dst, phase, l):
        def one(t, _):
            k = lax.rem(q + t, 4)
            xd, cd = lax.div(k, 2), lax.rem(k, 2)
            remote(src_of(k, xd, cd), dst, phase, l, dev(j, xd, cd, z)).start()
            return 0

        lax.fori_loop(1, 4, one, 0)

    def level(l, _):
        wait(recv.at[C, l], crecv.at[l])
        top, bottom = rows(l, crecv[l].reshape(nx, kc))
        field[l, 0] = top.reshape(zn, 2, hr, kc)
        field[l, 1] = bottom.reshape(zn, 2, hr, kc)
        to_plane(lambda k, xd, cd: field.at[l, xd, :, cd], gx.at[l, q], GX, l)
        gx[l, q] = field[l, xl, :, core]
        wait(recv.at[GX, l], gx.at[l, pl.ds(0, 3)])
        x = jnp.concatenate([gx[l, k].reshape(zn * hr, kc) for k in range(4)], axis=1)
        alpha = times_table(x, icol).reshape(zn, an, 8, ny)
        wait(recv.at[E, l], erecv.at[l])
        for a in range(an):
            for b in range(bn):
                lanes = slice(b * lw, (b + 1) * lw)
                prod[l, a * bn + b] = alpha[:, a, :, lanes] * erecv[l, :, a, :, lanes]

        def to_group(t, _):
            jd = lax.rem(j + t, jn)
            remote(prod.at[l, jd], rs1.at[l, j], RS1, l, dev(jd, xl, core, z)).start()
            return 0

        lax.fori_loop(1, jn, to_group, 0)
        rs1[l, j] = prod[l, j]
        wait(recv.at[RS1, l], rs1.at[l, pl.ds(0, jn - 1)])
        part[l] = jnp.sum(rs1[l], axis=0)

        def to_z(t, _):
            zd = lax.rem(z + t, zn)
            remote(part.at[l, zd], rs2.at[l, z], RS2, l, dev(j, xl, core, zd)).start()
            return 0

        lax.fori_loop(1, zn, to_z, 0)
        rs2[l, z] = part[l, z]
        wait(recv.at[RS2, l], rs2.at[l, pl.ds(0, zn - 1)])
        total = jnp.sum(rs2[l], axis=0)

        first = core * hr + lax.div(j, bn) * 8
        first = pl.multiple_of(first, 8)
        lane = pl.multiple_of(lax.rem(j, bn) * lw, lw)
        here = lax.broadcasted_iota(jnp.int32, (8, rn), 0) + first == lax.broadcasted_iota(jnp.int32, (8, rn), 1)
        scale = jnp.sum(jnp.where(here, rscale[pl.ds(l, 1), :], 0.0), axis=1, keepdims=True) * factor
        weighted = prec[l, pl.ds(first, 8), pl.ds(lane, lw)] * (
            scale * total - innov[l, pl.ds(first, 8), pl.ds(lane, lw)]
        )
        wz[l, z] = scale * weighted

        def w_to_z(t, _):
            remote(wz.at[l, z], wz.at[l, z], WZ, l, dev(j, xl, core, lax.rem(z + t, zn))).start()
            return 0

        lax.fori_loop(1, zn, w_to_z, 0)
        wait(recv.at[WZ, l], wz.at[l, pl.ds(0, zn - 1)])
        to_groups(wz.at[l], wg.at[l, j], WG, l)
        wg[l, j] = wz[l]
        wait(recv.at[WG, l], wg.at[l, pl.ds(0, jn - 1)])

        for a in range(an):
            for b in range(bn):
                lanes = slice(b * lw, (b + 1) * lw)
                adj[:, a, :, lanes] = wg[l, a * bn + b] * erecv[l, :, a, :, lanes]
        y = times_table(adj[...].reshape(zn * hr, ny), col)
        for k in range(4):
            adjc[l, k] = y[:, k * kc : (k + 1) * kc].reshape(zn, hr, kc)
        to_plane(lambda k, xd, cd: adjc.at[l, k], ax.at[l, xl, :, core], AX, l)
        ax[l, xl, :, core] = adjc[l, q]
        wait(recv.at[AX, l], adjc.at[l, pl.ds(0, 3)])
        top, bottom = rows(l, ax[l].reshape(nx, kc))
        gout[l, 0] = top.reshape(zn, rn, kc)
        gout[l, 1] = bottom.reshape(zn, rn, kc)

        def send_g(t, _):
            xd = lax.rem(t, 2)
            zd = lax.rem(lax.div(t, 2) + z, zn)
            same = in_plane_set & (xd == xl) & (zd == z)
            either(same, gout.at[l, xd, zd], grecv.at[l, member, q], G, l, dev(j, xd, owner_core, zd))
            return 0

        lax.fori_loop(0, 2 * zn, send_g, 0)
        return 0

    lax.fori_loop(0, 2, level, 0)

    def finish(l, _):
        wait(recv.at[G, l], grecv.at[l])
        x = jnp.concatenate([grecv[l, :, k].reshape(mn * rn, kc) for k in range(4)], axis=1)
        out[:, l] = ctrl[:, l] + times_table(x, icol).reshape(mn, rn, ny)
        return 0

    lax.fori_loop(0, 2, finish, 0)

    wait(send.at[SPZ, 0], specz.at[:, pl.ds(0, zn - 1)])
    wait(send.at[SPG, 0], specg.at[pl.ds(0, jn - 1)])

    def sent(l, _):
        wait(send.at[GX, l], gx.at[l, pl.ds(0, 3)])
        wait(send.at[AX, l], adjc.at[l, pl.ds(0, 3)])
        wait(send.at[RS1, l], rs1.at[l, pl.ds(0, jn - 1)])
        wait(send.at[WG, l], wg.at[l, pl.ds(0, jn - 1)])
        wait(send.at[RS2, l], rs2.at[l, pl.ds(0, zn - 1)])
        wait(send.at[WZ, l], wz.at[l, pl.ds(0, zn - 1)])

        @pl.when(in_plane_set)
        def _():
            wait(send.at[C, l], crecv.at[l, 0])
            wait(send.at[C, l], crecv.at[l, 1, pl.ds(0, zn - 1)])
            wait(send.at[E, l], erecv.at[l, pl.ds(0, zn - 1)])
            wait(send.at[G, l], gout.at[l, 0])
            wait(send.at[G, l], gout.at[l, 1, pl.ds(0, zn - 1)])

        @pl.when(jnp.logical_not(in_plane_set))
        def _():
            wait(send.at[C, l], crecv.at[l])
            wait(send.at[E, l], erecv.at[l])
            wait(send.at[G, l], gout.at[l])

        return 0

    lax.fori_loop(0, 2, sent, 0)


def body(zn, jn, members_all, interpret_lanes, ensemble, control, spectrum, row_scale, precision, innovation):
    mn, _, rn, ny = control.shape
    nx = spectrum.shape[2]
    kb = spectrum.shape[1] // 2
    kc, hr, px = ny // 4, rn // 2, nx // jn
    lw = interpret_lanes
    an = hr // 8
    assert mn * 2 == zn and an * (ny // lw) == jn and kb * zn == kc
    h_col, h_row = hartley_matrix(ny), hartley_matrix(nx)
    k = np.arange(ny).reshape(2, zn, 2, kb).transpose(0, 2, 1, 3).reshape(-1)
    col, icol = two_parts(h_col[:, k]), two_parts(h_col[k, :])
    even, odd = h_row[0::2, : nx // 2], h_row[1::2, : nx // 2]
    row = np.stack([two_parts(even), two_parts(odd), two_parts(odd.T)])
    f32 = jnp.float32
    vmem, anyspace = pl.BlockSpec(memory_space=pltpu.VMEM), pl.BlockSpec(memory_space=pl.ANY)
    return pl.pallas_call(
        functools.partial(kernel, zn, jn, 1.0 / math.sqrt(members_all - 1)),
        out_shape=jax.ShapeDtypeStruct(control.shape, f32),
        in_specs=[vmem] * 8 + [anyspace],
        out_specs=vmem,
        scratch_shapes=[
            pltpu.VMEM(row.shape, jnp.bfloat16),
            pltpu.VMEM((2, mn, 4, rn, kc), f32),
            pltpu.VMEM((2, 2, zn, rn, kc), f32),
            pltpu.VMEM((2, mn, 2, an, 8, ny), f32),
            pltpu.VMEM((2, zn, an, 8, ny), f32),
            pltpu.VMEM((2, zn, kb, px), f32),
            pltpu.VMEM((jn, 2, zn, kb, px), f32),
            pltpu.VMEM((2, nx, kc), f32),
            pltpu.VMEM((2, 2, zn, 2, hr, kc), f32),
            pltpu.VMEM((2, 4, zn, hr, kc), f32),
            pltpu.VMEM((2, jn, zn, 8, lw), f32),
            pltpu.VMEM((2, jn, zn, 8, lw), f32),
            pltpu.VMEM((2, zn, 8, lw), f32),
            pltpu.VMEM((2, zn, 8, lw), f32),
            pltpu.VMEM((2, zn, 8, lw), f32),
            pltpu.VMEM((2, jn, zn, 8, lw), f32),
            pltpu.VMEM((zn, an, 8, ny), f32),
            pltpu.VMEM((2, 4, zn, hr, kc), f32),
            pltpu.VMEM((2, 2, zn, 2, hr, kc), f32),
            pltpu.VMEM((2, 2, zn, rn, kc), f32),
            pltpu.VMEM((2, mn, 4, rn, kc), f32),
            pltpu.SemaphoreType.DMA((11, 2)),
            pltpu.SemaphoreType.DMA((11, 2)),
            pltpu.SemaphoreType.DMA,
        ],
        compiler_params=pltpu.CompilerParams(
            collective_id=0, has_side_effects=True, vmem_limit_bytes=50 * 1024 * 1024
        ),
        name="gradient",
    )(control, ensemble, spectrum, row_scale, precision, innovation, jnp.asarray(col), jnp.asarray(icol), jnp.asarray(row))


def solution(mesh, lanes=128):
    zn, jn = mesh.shape["space"] // 2, mesh.shape["ens"] // 2
    in_specs = (
        P("ens", None, "space", None),
        P("ens", None, "space", None),
        P(None, "space", None),
        P(None, "space"),
        P(None, "space", None),
        P(None, "space", None),
    )
    out_specs = P("ens", None, "space", None)

    def whole(ensemble, *rest):
        step = functools.partial(body, zn, jn, ensemble.shape[0], lanes)
        return jax.shard_map(step, mesh=mesh, in_specs=in_specs, out_specs=out_specs, check_vma=False)(ensemble, *rest)

    return whole
```

time: 720 us -> 235 us (0.33); the launches traced: 709 us -> 234 us
  blocking collectives: 247 us -> 0 us
  Pallas kernels: 0 us -> 226 us
  waiting for transfers between devices: 150 us -> 0 us
  matrix products: 141 us -> 0 us
  local copies, waits for them, and re-layouts: 144 us -> 7.85 us
  between operations: 13.8 us -> 0.02 us
  other arithmetic: 13.7 us -> 0 us
    all_to_all x4 -> x0, blocking collectives: 247 us -> none  [the longest x2 129 us: localize(): lax.all_to_all(columns, 'space', split_axis=2, concat_axis=3, tiled=True)]
    pallas_call x0 -> x1, Pallas kernels: none -> 226 us  [body(): pl.pallas_call(functools.partial(kernel, zn, jn, 1.0 / math.sqrt(members_...]
    psum x1 -> x0, waiting for transfers between devices: 150 us -> none  [body(): total = lax.psum(partial_sum, 'ens')]
    dot_general x8 -> x0, matrix products: 141 us -> none  [the longest x2 43.3 us: localize(): jnp.einsum('mlkr,rq->mlkq', columns, row_table, precision=HIGH)]
    unnamed x20 -> x15, local copies, waits for them, and re-layouts: 72.8 us -> 7.85 us
    all_to_all x9 -> x0, local copies, waits for them, and re-layouts: 44.8 us -> none  [the longest x2 23.2 us: localize(): lax.all_to_all(rows, 'space', split_axis=3, concat_axis=2, tiled=True)]
    dot_general x2 -> x0, local copies, waits for them, and re-layouts: 17.4 us -> none  [localize(): rows = jnp.einsum('mlkq,qr->mlkr', rows, row_table, precision=HIGH)]
    all_to_all x4 -> x0, other arithmetic: 12.7 us -> none  [the longest x2 6.35 us: localize(): lax.all_to_all(rows, 'space', split_axis=3, concat_axis=2, tiled=True)]
  transfers between devices with their start and end apart: 1 -> 0, of which waited for: 1 -> 0; matrix products, arithmetic and copies ran while one was open for 0% -> 0% of each run, Pallas kernels for 0% -> 0%
where the time goes in v1:
time: 235 us; the launch traced here: 234 us
  Pallas kernels  226 us (96%)
  local copies, waits for them, and re-layouts  7.85 us (3%)
    pallas_call x1, Pallas kernels, body(): pl.pallas_call(functools.partial(kernel, zn, jn, 1.0 / math.sqrt(members_...  226 us
    unnamed x15, local copies, waits for them, and re-layouts  7.85 us

profile of v1, /device:TPU:1, one launch (start us, length us, event | category | flops | bytes accessed | tf_op | source)
XLA Modules:
  0.0 234.2 jit_solution(1460171823806328033)
XLA Ops:
  0.0 0.0 copy-start
  0.0 1.2 copy-done
  1.2 0.0 copy-start.1
  1.2 1.2 copy-done.1
  2.5 0.0 copy-start.2
  2.5 1.0 copy-done.2
  3.5 0.0 copy-start.3
  3.5 0.9 copy-done.3
  4.4 0.0 copy-start.4
  4.4 0.9 copy-done.4
  5.3 0.0 copy-start.5
  5.3 0.9 copy-done.5
  6.2 0.0 copy-start.6
  6.2 0.7 copy-done.6
  6.9 226.3 %gradient.1 = f32[8,2,32,512]{3,2,1,0:T(8,128)S(1)} custom-call(f32[8,2,32,512]{3,2,1,0:T(8,128)S(1)} %copy-done, bf16[8,2,32,512]{3,2,1,0:T(8,128)(2,1)S(1)} %copy-done.2, f32[2,16,1024]{2,1,0:T(8,128)S(1)} %copy-done.3, f32[2,32]{1,0:T(2,128)S(1)} %copy-done.6, f32[2,32,512]{2,1,0:T(8,128)S(1)} %copy-done.4, f32[2,32,512]{2,1,0:T(8,128)S(1)} %copy-done.5, ...), custom_call_target="tpu_custom_call" | custom-call | tf_op jit(solution)/shard_map/gradient/pallas_call | solution.py:327
  233.2 1.0 copy.11
Async XLA Ops:
  0.0 1.2 copy-start
  1.2 1.2 copy-start.1
  2.5 1.0 copy-start.2
  3.5 0.9 copy-start.3
  4.4 0.9 copy-start.4
  5.3 0.9 copy-start.5
  6.2 0.7 copy-start.6

commit v2 on v1

v2 whole, which is shorter than its diff:
```python
import functools
import math

import jax
import jax.numpy as jnp
import ml_dtypes
import numpy as np
from jax import lax
from jax.experimental import pallas as pl
from jax.experimental.pallas import tpu as pltpu
from jax.sharding import PartitionSpec as P

MESH = pl.DeviceIdType.MESH
SPZ, SPG, C, E, GX, RS1, RS2, WZ, WG, AX, G = range(11)
FEED = ((2, 4, 9, 20, 32), (2, 3, 6, 16, 16))


def hartley_matrix(n):
    index = np.arange(n, dtype=np.int64)
    angle = (index[:, None] * index[None, :] % n) * (2.0 * math.pi / n)
    return (np.cos(angle) + np.sin(angle)) / math.sqrt(n)


def two_parts(table):
    high = table.astype(ml_dtypes.bfloat16)
    low = (table - high.astype(np.float64)).astype(ml_dtypes.bfloat16)
    return np.stack([high, low])


def dot(a, b):
    return jnp.dot(a, b, preferred_element_type=jnp.float32)


def parts_of(x):
    high = x.astype(jnp.bfloat16)
    return high, (x - high.astype(jnp.float32)).astype(jnp.bfloat16)


def times_table(x, table):
    high, low = parts_of(x)
    return dot(high, table[0]) + dot(low, table[0]) + dot(high, table[1])


def table_times(table, k, y):
    high, low = parts_of(y)
    width = y.shape[1]
    both = dot(table[k, 0], jnp.concatenate([high, low], axis=1))
    return both[:, :width] + both[:, width:] + dot(table[k, 1], high)


def kernel(
    zn, jn, factor,
    ctrl_hbm, ens_hbm, spec_hbm, rscale_hbm, prec_hbm, innov_hbm, col_hbm, icol_hbm, row_hbm,
    out,
    ctrl, ens, spec, rscale, prec, innov, col, icol, row,
    cst, crecv, e32, erecv, specz, specg, spect, field, gx, alpha, prod, rs1, part, rs2, wz, wg, adj, adjc, ax, nat, gout,
    grecv, send, recv, local_sem,
):
    mn, _, rn, ny = ctrl.shape
    nx = spec.shape[2]
    kb = spec.shape[1] // 2
    kc = ny // 4
    hr = rn // 2
    half = nx // 2
    lw = prod.shape[4]
    bn = ny // lw
    an = jn // bn
    px = nx // jn
    chunks = min(4, zn)
    cs = zn // chunks
    ei, si = lax.axis_index("ens"), lax.axis_index("space")
    j, core = lax.div(ei, 2), lax.rem(ei, 2)
    xl, z = lax.div(si, zn), lax.rem(si, zn)
    q = xl * 2 + core
    owner_core = lax.div(z, mn)
    member = lax.rem(z, mn)
    in_plane_set = owner_core == core

    def dev(j_, xl_, core_, z_):
        return (j_ * 2 + core_, xl_ * zn + z_)

    def remote(src, dst, phase, l, device, c=0):
        return pltpu.make_async_remote_copy(
            src_ref=src, dst_ref=dst, send_sem=send.at[phase, l], recv_sem=recv.at[phase, l, c],
            device_id=device, device_id_type=MESH,
        )

    def wait(sem, ref):
        pltpu.make_async_copy(ref, ref, sem).wait()

    def offset(p):
        far = lax.div(zn - p, 2)
        return jnp.where(lax.rem(p, 2) == 1, far, -far)

    def plane_of(p):
        return lax.rem(z + offset(p) + zn, zn)

    def plane_back(p):
        return lax.rem(z - offset(p) + zn, zn)

    loads = [
        pltpu.make_async_copy(src, dst, local_sem.at[i])
        for i, (src, dst) in enumerate(
            [
                (ctrl_hbm.at[:, 0], ctrl.at[:, 0]), (col_hbm, col), (spec_hbm, spec), (ens_hbm, ens),
                (ctrl_hbm.at[:, 1], ctrl.at[:, 1]), (row_hbm, row), (icol_hbm, icol), (rscale_hbm, rscale),
                (prec_hbm, prec), (innov_hbm, innov),
            ]
        )
    ]
    barrier = pltpu.get_barrier_semaphore()
    mine = q * zn + z

    def greet_group(t, _):
        other = lax.rem(mine + t, 4 * zn)
        oq, oz = lax.div(other, zn), lax.rem(other, zn)
        pl.semaphore_signal(barrier, inc=1, device_id=dev(j, lax.div(oq, 2), lax.rem(oq, 2), oz), device_id_type=MESH)
        return 0

    lax.fori_loop(1, 4 * zn, greet_group, 0)

    def greet_others(t, _):
        pl.semaphore_signal(barrier, inc=1, device_id=dev(lax.rem(j + t, jn), xl, core, z), device_id_type=MESH)
        return 0

    lax.fori_loop(1, jn, greet_others, 0)
    for load in loads[:5]:
        load.start()

    def columns(l):
        y = times_table(ctrl[:, l].reshape(mn * rn, ny), col)
        for k in range(4):
            cst[l, :, k] = y[:, k * kc : (k + 1) * kc].reshape(mn, rn, kc)

    def widen(l):
        for m in range(mn):
            e32[l, m] = ens[m, l].astype(jnp.float32).reshape(2, an, 8, ny)

    def either(same, src, dst, phase, l, device, c=0):
        @pl.when(same)
        def _():
            pltpu.make_async_copy(src, dst, recv.at[phase, l, c]).start()

        @pl.when(jnp.logical_not(same))
        def _():
            remote(src, dst, phase, l, device, c).start()

    def send_control(l, low, high):
        def one(p, _):
            zd = plane_back(p)

            @pl.when(lax.div(zd, mn) == core)
            def _():
                for k in range(4):
                    remote(cst.at[l, lax.rem(zd, mn), k], crecv.at[l, xl, z], C, l, dev(j, k // 2, k % 2, zd)).start()

            return 0

        lax.fori_loop(low, min(high, zn - 1), one, 0)
        if low < high == zn:

            @pl.when(in_plane_set)
            def _():
                for k in range(4):
                    either(q == k, cst.at[l, member, k], crecv.at[l, xl, z], C, l, dev(j, k // 2, k % 2, z))

    def send_ensemble(l, low, high):
        def one(p, _):
            zd = plane_back(p)

            @pl.when(lax.div(zd, mn) == core)
            def _():
                for k in range(2):
                    remote(
                        e32.at[l, lax.rem(zd, mn), k], erecv.at[l, p], E, l, dev(j, xl, k, zd), lax.div(p, cs)
                    ).start()

            return 0

        lax.fori_loop(low, min(high, zn - 1), one, 0)
        if low < high == zn:

            @pl.when(in_plane_set)
            def _():
                for k in range(2):
                    either(core == k, e32.at[l, member, k], erecv.at[l, zn - 1], E, l, dev(j, xl, k, z), chunks - 1)

    def send_gradient(l, low, high):
        def one(p, _):
            zd = plane_back(p)
            for k in range(2):
                remote(gout.at[l, k, zd], grecv.at[l, member, q], G, l, dev(j, k, owner_core, zd)).start()
            return 0

        lax.fori_loop(low, min(high, zn - 1), one, 0)
        if low < high == zn:
            for k in range(2):
                either(
                    in_plane_set & (xl == k), gout.at[l, k, z], grecv.at[l, member, q], G, l, dev(j, k, owner_core, z)
                )

    def to_groups(src_of, dst, phase, l, c=0):
        def one(t, _):
            jd = lax.rem(j + t, jn)
            remote(src_of(jd), dst, phase, l, dev(jd, xl, core, z), c).start()
            return 0

        lax.fori_loop(1, jn, one, 0)

    def to_plane(src_of, dst, phase, l, c=0):
        def one(t, _):
            k = lax.rem(q + t, 4)
            xd, cd = lax.div(k, 2), lax.rem(k, 2)
            remote(src_of(k, xd, cd), dst, phase, l, dev(j, xd, cd, z), c).start()
            return 0

        lax.fori_loop(1, 4, one, 0)

    def rows(l, y):
        even = table_times(row, 0, y[:half] + y[half:]) * spect[l, pl.ds(0, half, 2), :]
        odd = table_times(row, 1, y[:half] - y[half:]) * spect[l, pl.ds(1, half, 2), :]
        a = table_times(row, 0, even)
        b = table_times(row, 2, odd)
        return a + b, a - b

    def start_alpha(l):
        wait(recv.at[C, l, 0], crecv.at[l])
        top, bottom = rows(l, crecv[l].reshape(nx, kc))
        field[l, 0] = top.reshape(zn, 2, hr, kc)
        field[l, 1] = bottom.reshape(zn, 2, hr, kc)
        to_plane(lambda k, xd, cd: field.at[l, xd, :, cd], gx.at[l, q], GX, l)
        gx[l, q] = field[l, xl, :, core]

    def make_alpha(l):
        wait(recv.at[GX, l, 0], gx.at[l, pl.ds(0, 3)])
        x = jnp.concatenate([gx[l, k].reshape(zn * hr, kc) for k in range(4)], axis=1)
        alpha[l] = times_table(x, icol).reshape(zn, an, 8, ny)

    def feed(l, point):
        low = FEED[l][point - 1] * zn // 16 if point else 0
        high = FEED[l][point] * zn // 16
        if l == 0:
            send_control(1, min(low, zn), min(high, zn))
            send_ensemble(1, max(low - zn, 0), max(high - zn, 0))
        else:
            send_gradient(0, low, high)

    def sum_groups(l, c):
        low, high = c * cs, (c + 1) * cs
        wait(recv.at[RS1, l, c], rs1.at[l, pl.ds(0, jn - 1), pl.ds(low, cs)])
        part[l, low:high] = jnp.sum(rs1[l, :, low:high], axis=0)

        def one(p, _):
            remote(part.at[l, p], rs2.at[l, p], RS2, l, dev(j, xl, core, plane_of(p))).start()
            return 0

        lax.fori_loop(low, min(high, zn - 1), one, 0)

    def sum_members(l):
        for c in range(chunks):
            low = c * cs
            if c >= chunks - 2:
                feed(l, c - (chunks - 2))
            wait(recv.at[E, l, c], erecv.at[l, pl.ds(low, cs)])

            def multiply(p, _):
                here = plane_of(p)
                for a in range(an):
                    for b in range(bn):
                        lanes = slice(b * lw, (b + 1) * lw)
                        prod[l, a * bn + b, p] = alpha[l, here, a, :, lanes] * erecv[l, p, a, :, lanes]
                return 0

            lax.fori_loop(low, low + cs, multiply, 0)
            to_groups(lambda jd: prod.at[l, jd, pl.ds(low, cs)], rs1.at[l, j, pl.ds(low, cs)], RS1, l, c)
            rs1[l, j, low : low + cs] = prod[l, j, low : low + cs]
            if c > 0:
                sum_groups(l, c - 1)
        sum_groups(l, chunks - 1)
        rs2[l, zn - 1] = part[l, zn - 1]

    def make_factor(l):
        wait(recv.at[RS2, l, 0], rs2.at[l, pl.ds(0, zn - 1)])
        total = jnp.sum(rs2[l], axis=0)
        first = pl.multiple_of(core * hr + lax.div(j, bn) * 8, 8)
        lane = pl.multiple_of(lax.rem(j, bn) * lw, lw)
        here = lax.broadcasted_iota(jnp.int32, (8, rn), 0) + first == lax.broadcasted_iota(jnp.int32, (8, rn), 1)
        scale = jnp.sum(jnp.where(here, rscale[l : l + 1, :], 0.0), axis=1, keepdims=True) * factor
        weighted = prec[l, pl.ds(first, 8), pl.ds(lane, lw)] * (
            scale * total - innov[l, pl.ds(first, 8), pl.ds(lane, lw)]
        )
        wz[l, zn - 1] = scale * weighted

        def one(p, _):
            remote(wz.at[l, zn - 1], wz.at[l, p], WZ, l, dev(j, xl, core, plane_back(p)), lax.div(p, cs)).start()
            return 0

        lax.fori_loop(0, zn - 1, one, 0)

    def spread_factor(l):
        for c in reversed(range(chunks)):
            low = c * cs
            others = cs - 1 if c == chunks - 1 else cs
            if others:
                wait(recv.at[WZ, l, c], wz.at[l, pl.ds(0, others)])
            to_groups(lambda jd: wz.at[l, pl.ds(low, cs)], wg.at[l, j, pl.ds(low, cs)], WG, l, c)
            wg[l, j, low : low + cs] = wz[l, low : low + cs]

    def start_adjoint(l):
        hs = zn // 2
        for h in (1, 0):
            low = h * hs
            for c in reversed(range(h * chunks // 2, (h + 1) * chunks // 2)):
                wait(recv.at[WG, l, c], wg.at[l, pl.ds(0, jn - 1), pl.ds(c * cs, cs)])
            for a in range(an):
                for b in range(bn):
                    lanes = slice(b * lw, (b + 1) * lw)
                    adj[low : low + hs, a, :, lanes] = (
                        wg[l, a * bn + b, low : low + hs] * erecv[l, low : low + hs, a, :, lanes]
                    )
            y = times_table(adj[low : low + hs].reshape(hs * hr, ny), col)
            for k in range(4):
                adjc[l, k, low : low + hs] = y[:, k * kc : (k + 1) * kc].reshape(hs, hr, kc)
            to_plane(
                lambda k, xd, cd: adjc.at[l, k, pl.ds(low, hs)], ax.at[l, xl, pl.ds(low, hs), core], AX, l, h
            )
            ax[l, xl, low : low + hs, core] = adjc[l, q, low : low + hs]

    def adjoint(l):
        hs = zn // 2
        for h in (1, 0):
            wait(recv.at[AX, l, h], adjc.at[l, pl.ds(0, 3), pl.ds(0, hs)])

        def place(p, _):
            nat[:, plane_of(p)] = ax[l, :, p]
            return 0

        lax.fori_loop(0, zn, place, 0)
        top, bottom = rows(l, nat[...].reshape(nx, kc))
        gout[l, 0] = top.reshape(zn, rn, kc)
        gout[l, 1] = bottom.reshape(zn, rn, kc)

    def finish(l):
        wait(recv.at[G, l, 0], grecv.at[l])
        x = jnp.concatenate([grecv[l, :, k].reshape(mn * rn, kc) for k in range(4)], axis=1)
        out[:, l] = ctrl[:, l] + times_table(x, icol).reshape(mn, rn, ny)

    loads[0].wait()
    loads[1].wait()
    columns(0)
    loads[2].wait()
    core_k = pl.multiple_of(core * kb, kb)
    piece = pl.multiple_of(j * px, px)
    specz[:, z] = spec[:, pl.ds(core_k, kb), pl.ds(piece, px)]
    pl.semaphore_wait(barrier, 4 * zn - 1 + jn - 1)

    def send_spec(t, _):
        remote(specz.at[:, z], specz.at[:, z], SPZ, 0, dev(j, xl, core, lax.rem(z + t, zn))).start()
        return 0

    lax.fori_loop(1, zn, send_spec, 0)
    send_control(0, 0, zn)
    loads[3].wait()
    widen(0)
    send_ensemble(0, 0, zn)
    for load in loads[5:]:
        load.start()
    loads[4].wait()
    columns(1)
    widen(1)
    for load in loads[5:]:
        load.wait()

    wait(recv.at[SPZ, 0, 0], specz.at[:, pl.ds(0, zn - 1)])
    to_groups(lambda jd: specz, specg.at[j], SPG, 0)
    specg[j] = specz[...]
    wait(recv.at[SPG, 0, 0], specg.at[pl.ds(0, jn - 1)])
    for l in range(2):
        for k in range(jn):
            spect[l, k * px : (k + 1) * px] = specg[k, l].reshape(kc, px).T

    start_alpha(0)
    make_alpha(0)
    for l in range(2):
        sum_members(l)
        feed(l, 2)
        make_factor(l)
        feed(l, 3)
        spread_factor(l)
        feed(l, 4)
        if l == 0:
            start_alpha(1)
        start_adjoint(l)
        if l == 0:
            make_alpha(1)
        adjoint(l)
    send_gradient(1, 0, zn)
    finish(0)
    finish(1)

    wait(send.at[SPZ, 0], specz.at[:, pl.ds(0, zn - 1)])
    wait(send.at[SPG, 0], specg.at[pl.ds(0, jn - 1)])

    def sent(l, _):
        wait(send.at[GX, l], gx.at[l, pl.ds(0, 3)])
        wait(send.at[AX, l], adjc.at[l, pl.ds(0, 3)])
        wait(send.at[RS1, l], rs1.at[l, pl.ds(0, jn - 1)])
        wait(send.at[WG, l], wg.at[l, pl.ds(0, jn - 1)])
        wait(send.at[RS2, l], rs2.at[l, pl.ds(0, zn - 1)])
        wait(send.at[WZ, l], wz.at[l, pl.ds(0, zn - 1)])

        @pl.when(in_plane_set)
        def _():
            wait(send.at[C, l], crecv.at[l, 0])
            wait(send.at[C, l], crecv.at[l, 1, pl.ds(0, zn - 1)])
            wait(send.at[E, l], erecv.at[l, pl.ds(0, zn - 1)])
            wait(send.at[G, l], gout.at[l, 0])
            wait(send.at[G, l], gout.at[l, 1, pl.ds(0, zn - 1)])

        @pl.when(jnp.logical_not(in_plane_set))
        def _():
            wait(send.at[C, l], crecv.at[l])
            wait(send.at[E, l], erecv.at[l])
            wait(send.at[G, l], gout.at[l])

        return 0

    lax.fori_loop(0, 2, sent, 0)


def body(zn, jn, members_all, interpret_lanes, ensemble, control, spectrum, row_scale, precision, innovation):
    mn, _, rn, ny = control.shape
    nx = spectrum.shape[2]
    kb = spectrum.shape[1] // 2
    kc, hr, px = ny // 4, rn // 2, nx // jn
    lw = interpret_lanes
    an = hr // 8
    assert mn * 2 == zn and an * (ny // lw) == jn and kb * zn == kc
    h_col, h_row = hartley_matrix(ny), hartley_matrix(nx)
    k = np.arange(ny).reshape(2, zn, 2, kb).transpose(0, 2, 1, 3).reshape(-1)
    col, icol = two_parts(h_col[:, k]), two_parts(h_col[k, :])
    even, odd = h_row[0::2, : nx // 2], h_row[1::2, : nx // 2]
    row = np.stack([two_parts(even), two_parts(odd), two_parts(odd.T)])
    f32 = jnp.float32
    vmem, anyspace = pl.BlockSpec(memory_space=pltpu.VMEM), pl.BlockSpec(memory_space=pl.ANY)
    return pl.pallas_call(
        functools.partial(kernel, zn, jn, 1.0 / math.sqrt(members_all - 1)),
        out_shape=jax.ShapeDtypeStruct(control.shape, f32),
        in_specs=[anyspace] * 9,
        out_specs=vmem,
        scratch_shapes=[
            pltpu.VMEM(control.shape, f32),
            pltpu.VMEM(ensemble.shape, ensemble.dtype),
            pltpu.VMEM(spectrum.shape, f32),
            pltpu.VMEM(row_scale.shape, f32),
            pltpu.VMEM(precision.shape, f32),
            pltpu.VMEM(innovation.shape, f32),
            pltpu.VMEM(col.shape, jnp.bfloat16),
            pltpu.VMEM(icol.shape, jnp.bfloat16),
            pltpu.VMEM(row.shape, jnp.bfloat16),
            pltpu.VMEM((2, mn, 4, rn, kc), f32),
            pltpu.VMEM((2, 2, zn, rn, kc), f32),
            pltpu.VMEM((2, mn, 2, an, 8, ny), f32),
            pltpu.VMEM((2, zn, an, 8, ny), f32),
            pltpu.VMEM((2, zn, kb, px), f32),
            pltpu.VMEM((jn, 2, zn, kb, px), f32),
            pltpu.VMEM((2, nx, kc), f32),
            pltpu.VMEM((2, 2, zn, 2, hr, kc), f32),
            pltpu.VMEM((2, 4, zn, hr, kc), f32),
            pltpu.VMEM((2, zn, an, 8, ny), f32),
            pltpu.VMEM((2, jn, zn, 8, lw), f32),
            pltpu.VMEM((2, jn, zn, 8, lw), f32),
            pltpu.VMEM((2, zn, 8, lw), f32),
            pltpu.VMEM((2, zn, 8, lw), f32),
            pltpu.VMEM((2, zn, 8, lw), f32),
            pltpu.VMEM((2, jn, zn, 8, lw), f32),
            pltpu.VMEM((zn, an, 8, ny), f32),
            pltpu.VMEM((2, 4, zn, hr, kc), f32),
            pltpu.VMEM((2, 2, zn, 2, hr, kc), f32),
            pltpu.VMEM((2, zn, 2, hr, kc), f32),
            pltpu.VMEM((2, 2, zn, rn, kc), f32),
            pltpu.VMEM((2, mn, 4, rn, kc), f32),
            pltpu.SemaphoreType.DMA((11, 2)),
            pltpu.SemaphoreType.DMA((11, 2, 4)),
            pltpu.SemaphoreType.DMA((10,)),
        ],
        compiler_params=pltpu.CompilerParams(
            collective_id=0, has_side_effects=True, vmem_limit_bytes=50 * 1024 * 1024
        ),
        name="gradient",
    )(control, ensemble, spectrum, row_scale, precision, innovation, jnp.asarray(col), jnp.asarray(icol), jnp.asarray(row))


def solution(mesh, lanes=128):
    zn, jn = mesh.shape["space"] // 2, mesh.shape["ens"] // 2
    in_specs = (
        P("ens", None, "space", None),
        P("ens", None, "space", None),
        P(None, "space", None),
        P(None, "space"),
        P(None, "space", None),
        P(None, "space", None),
    )
    out_specs = P("ens", None, "space", None)

    def whole(ensemble, *rest):
        step = functools.partial(body, zn, jn, ensemble.shape[0], lanes)
        return jax.shard_map(step, mesh=mesh, in_specs=in_specs, out_specs=out_specs, check_vma=False)(ensemble, *rest)

    return whole
```

time: 235 us -> 212 us (0.902)
  Pallas kernels: 226 us -> 203 us
    pallas_call x1, Pallas kernels: 226 us -> 203 us  [body(): pl.pallas_call(functools.partial(kernel, zn, jn, 1.0 / math.sqrt(members_...]
where the time goes in v2:
time: 212 us; the launch traced here: 211 us
  Pallas kernels  203 us (96%)
  local copies, waits for them, and re-layouts  7.85 us (4%)
    pallas_call x1, Pallas kernels, body(): pl.pallas_call(functools.partial(kernel, zn, jn, 1.0 / math.sqrt(members_...  203 us
    unnamed x15, local copies, waits for them, and re-layouts  7.85 us

profile of v2, /device:TPU:1, one launch (start us, length us, event | category | flops | bytes accessed | tf_op | source)
XLA Modules:
  0.0 211.4 jit_solution(13726936106588955583)
XLA Ops:
  0.0 0.0 copy-start
  0.0 1.2 copy-done
  1.2 0.0 copy-start.1
  1.2 1.2 copy-done.1
  2.5 0.0 copy-start.2
  2.5 1.0 copy-done.2
  3.5 0.0 copy-start.3
  3.5 0.9 copy-done.3
  4.4 0.0 copy-start.4
  4.4 0.9 copy-done.4
  5.3 0.0 copy-start.5
  5.3 0.9 copy-done.5
  6.2 0.0 copy-start.6
  6.2 0.7 copy-done.6
  6.9 203.5 %gradient.1 = f32[8,2,32,512]{3,2,1,0:T(8,128)S(1)} custom-call(f32[8,2,32,512]{3,2,1,0:T(8,128)S(1)} %copy-done, bf16[8,2,32,512]{3,2,1,0:T(8,128)(2,1)S(1)} %copy-done.2, f32[2,16,1024]{2,1,0:T(8,128)S(1)} %copy-done.3, f32[2,32]{1,0:T(2,128)S(1)} %copy-done.6, f32[2,32,512]{2,1,0:T(8,128)S(1)} %copy-done.4, f32[2,32,512]{2,1,0:T(8,128)S(1)} %copy-done.5, ...), custom_call_target="tpu_custom_call" | custom-call | tf_op jit(solution)/shard_map/gradient/pallas_call | solution.py:446
  210.4 1.0 copy.11
Async XLA Ops:
  0.0 1.2 copy-start
  1.2 1.2 copy-start.1
  2.5 1.0 copy-start.2
  3.5 0.9 copy-start.3
  4.4 0.9 copy-start.4
  5.3 0.9 copy-start.5
  6.2 0.7 copy-start.6

commit v3 on v2

--- a/solution.py
+++ b/solution.py
@@ -12,7 +12,7 @@
 
 MESH = pl.DeviceIdType.MESH
 SPZ, SPG, C, E, GX, RS1, RS2, WZ, WG, AX, G = range(11)
-FEED = ((2, 4, 9, 20, 32), (2, 3, 6, 16, 16))
+FEED = ((4, 6, 12, 32, 32), (0, 0, 0, 16, 16))
 
 
 def hartley_matrix(n):
@@ -66,7 +66,7 @@
     bn = ny // lw
     an = jn // bn
     px = nx // jn
-    chunks = min(4, zn)
+    chunks = min(2, zn)
     cs = zn // chunks
     ei, si = lax.axis_index("ens"), lax.axis_index("space")
     j, core = lax.div(ei, 2), lax.rem(ei, 2)
@@ -381,19 +381,24 @@
 
     start_alpha(0)
     make_alpha(0)
-    for l in range(2):
-        sum_members(l)
-        feed(l, 2)
-        make_factor(l)
-        feed(l, 3)
-        spread_factor(l)
-        feed(l, 4)
-        if l == 0:
-            start_alpha(1)
-        start_adjoint(l)
-        if l == 0:
-            make_alpha(1)
-        adjoint(l)
+    sum_members(0)
+    feed(0, 2)
+    make_factor(0)
+    feed(0, 3)
+    spread_factor(0)
+    feed(0, 4)
+    start_alpha(1)
+    start_adjoint(0)
+    make_alpha(1)
+    sum_members(1)
+    adjoint(0)
+    feed(1, 2)
+    make_factor(1)
+    feed(1, 3)
+    spread_factor(1)
+    feed(1, 4)
+    start_adjoint(1)
+    adjoint(1)
     send_gradient(1, 0, zn)
     finish(0)
     finish(1)
@@ -485,7 +490,7 @@
             pltpu.SemaphoreType.DMA((10,)),
         ],
         compiler_params=pltpu.CompilerParams(
-            collective_id=0, has_side_effects=True, vmem_limit_bytes=50 * 1024 * 1024
+            collective_id=0, has_side_effects=True, vmem_limit_bytes=63 * 1024 * 1024
         ),
         name="gradient",
     )(control, ensemble, spectrum, row_scale, precision, innovation, jnp.asarray(col), jnp.asarray(icol), jnp.asarray(row))

time: 212 us -> 199 us (0.939)
  Pallas kernels: 203 us -> 196 us
  local copies, waits for them, and re-layouts: 7.85 us -> 2.29 us
    pallas_call x1, Pallas kernels: 203 us -> 196 us  [body(): pl.pallas_call(functools.partial(kernel, zn, jn, 1.0 / math.sqrt(members_...]
    unnamed x15 -> x1, local copies, waits for them, and re-layouts: 7.85 us -> 2.29 us
where the time goes in v3:
time: 199 us; the launch traced here: 198 us
  Pallas kernels  196 us (98%)
  local copies, waits for them, and re-layouts  2.29 us (1%)
    pallas_call x1, Pallas kernels, body(): pl.pallas_call(functools.partial(kernel, zn, jn, 1.0 / math.sqrt(members_...  196 us

profile of v3, /device:TPU:1, one launch (start us, length us, event | category | flops | bytes accessed | tf_op | source)
XLA Modules:
  0.0 198.4 jit_solution(14069721465162672104)
XLA Ops:
  0.0 196.1 %gradient.1 = f32[8,2,32,512]{3,2,1,0:T(8,128)} custom-call(f32[8,2,32,512]{3,2,1,0:T(8,128)} %ctrl_hbm.1, bf16[8,2,32,512]{3,2,1,0:T(8,128)(2,1)} %ens_hbm.1, f32[2,16,1024]{2,1,0:T(8,128)} %spec_hbm.1, f32[2,32]{1,0:T(2,128)} %rscale_hbm.1, f32[2,32,512]{2,1,0:T(8,128)} %prec_hbm.1, f32[2,32,512]{2,1,0:T(8,128)} %innov_hbm.1, ...), custom_call_target="tpu_custom_call" | custom-call | tf_op jit(solution)/shard_map/gradient/pallas_call | solution.py:451
  196.1 2.3 %copy.11 = f32[8,2,32,512]{3,2,1,0:T(8,128)} copy(f32[8,2,32,512]{3,2,1,0:T(8,128)} %gradient.1) | data formatting | bytes 2097152

commit v4 on v3

--- a/solution.py
+++ b/solution.py
@@ -12,7 +12,7 @@
 
 MESH = pl.DeviceIdType.MESH
 SPZ, SPG, C, E, GX, RS1, RS2, WZ, WG, AX, G = range(11)
-FEED = ((4, 6, 12, 32, 32), (0, 0, 0, 16, 16))
+FEED = ((2, 3, 13, 32, 32), (0, 0, 0, 16, 16))
 
 
 def hartley_matrix(n):

time: 199 us -> 198 us (level)
  Pallas kernels: 196 us -> 194 us
    pallas_call x1, Pallas kernels: 196 us -> 194 us  [body(): pl.pallas_call(functools.partial(kernel, zn, jn, 1.0 / math.sqrt(members_...]
where the time goes in v4:
time: 198 us; the launch traced here: 196 us
  Pallas kernels  194 us (98%)
  local copies, waits for them, and re-layouts  2.29 us (1%)
    pallas_call x1, Pallas kernels, body(): pl.pallas_call(functools.partial(kernel, zn, jn, 1.0 / math.sqrt(members_...  194 us

profile of v4, /device:TPU:1, one launch (start us, length us, event | category | flops | bytes accessed | tf_op | source)
XLA Modules:
  0.0 196.4 jit_solution(18293970915807485612)
XLA Ops:
  0.0 194.1 %gradient.1 = f32[8,2,32,512]{3,2,1,0:T(8,128)} custom-call(f32[8,2,32,512]{3,2,1,0:T(8,128)} %ctrl_hbm.1, bf16[8,2,32,512]{3,2,1,0:T(8,128)(2,1)} %ens_hbm.1, f32[2,16,1024]{2,1,0:T(8,128)} %spec_hbm.1, f32[2,32]{1,0:T(2,128)} %rscale_hbm.1, f32[2,32,512]{2,1,0:T(8,128)} %prec_hbm.1, f32[2,32,512]{2,1,0:T(8,128)} %innov_hbm.1, ...), custom_call_target="tpu_custom_call" | custom-call | tf_op jit(solution)/shard_map/gradient/pallas_call | solution.py:451
  194.1 2.3 %copy.11 = f32[8,2,32,512]{3,2,1,0:T(8,128)} copy(f32[8,2,32,512]{3,2,1,0:T(8,128)} %gradient.1) | data formatting | bytes 2097152
